TPU v7x, 768 devices: a whole 4x8x12 slice. The times are simulated.
768 devices in a mesh: outer: 4 (over x_hi, core), rep: 16 (over y, x_lo), exp: 12 (over z).
Axes of the slice: x: 4 (x_hi: 2, x_lo: 2; x = x_hi * 2 + x_lo), y: 8, z: 12, core: 2. Of those that a mesh axis runs over, the one named last changes fastest.
Arguments:
- saved_hidden: bfloat16 [4, 16, 4608, 512], P('outer', 'rep', 'exp'), may hold values from -6 to 6
- routed_grad: bfloat16 [4, 16, 4608, 2048], P('outer', 'rep', 'exp'), may hold values from -0.19921875 to 0.19921875
- expert_counts: int32 [4, 16, 24], P('outer', 'rep', 'exp'), may hold values from 0 to 384, as said below
- block_starts: int32 [4, 16, 24], P('outer', 'rep', 'exp'), may hold values from 0 to 3
- master_weights: float32 [24, 2048, 512], P('exp', 'rep', 'outer'), may hold values from -0.0125 to 0.0125
- first_moment: float32 [24, 2048, 512], P('exp', 'rep', 'outer'), may hold values from -0.9 to 0.9
- second_moment: float32 [24, 2048, 512], P('exp', 'rep', 'outer'), may hold values from 0.01 to 1
Outputs:
- new_master: float32 [24, 2048, 512], P('exp', 'rep', 'outer')
- new_first: float32 [24, 2048, 512], P('exp', 'rep', 'outer')
- new_second: float32 [24, 2048, 512], P('exp', 'rep', 'outer')
- new_weights: bfloat16 [24, 2048, 512], P('exp')
Inputs may be any that keep to these rules, and one draw needn't show every extreme that they name: On each device, the rows of its local expert e are rows 128 * block_starts[e] to 128 * block_starts[e] + expert_counts[e] - 1 of its 384 expert-side rows; the local experts come in increasing order of e, each in whole blocks of 128 rows of its own that no other expert touches, all within the device's 3 blocks; other rows belong to no expert. In every draw some device gives all its 3 blocks to one expert.
All inputs are finite; a program needn't handle non-finite values.
Results may differ from a plain program's by a relative error of at most 0.015.
Values may be sent and summed in bfloat16 or wider, within the bound.
A program may use at most 32 MiB of HBM per device.

v0:
```python
import jax
import jax.numpy as jnp
from jax import lax
from jax.sharding import PartitionSpec as P

BLOCK = 128


beta_one = 0.9
beta_two = 0.95
learn_rate = 0.001
decay_rate = 0.1
epsilon = 1e-08
correct_one = 0.9999734386011124
correct_two = 0.994079470779666


def cut_along(x, dim, length):
    shape = x.shape
    parts = x.reshape(*shape[:dim], length, shape[dim] // length, *shape[dim + 1 :])
    return jnp.moveaxis(parts, dim, 0)


def summed_on_arrival(x, axis, dim):
    parts = cut_along(x, dim, lax.axis_size(axis))
    arrived = lax.all_to_all(parts, axis, split_axis=0, concat_axis=0, tiled=True)
    return arrived.astype(jnp.float32).sum(axis=0)


def sent_to_all(x, axis):
    copies = jnp.broadcast_to(x, (lax.axis_size(axis), *x.shape))
    return lax.all_to_all(copies, axis, split_axis=0, concat_axis=0, tiled=True)


def joined_along(parts, dim):
    shape = list(parts.shape[1:])
    shape[dim] *= parts.shape[0]
    return jnp.moveaxis(parts, 0, dim).reshape(shape)


def gather_directly(x, axis, dim):
    parts = sent_to_all(x, axis)
    return joined_along(parts, dim)


def adamw(grad_part, master, moment_one, moment_two):
    new_one = beta_one * moment_one + (1.0 - beta_one) * grad_part
    new_two = beta_two * moment_two + (1.0 - beta_two) * grad_part * grad_part
    update = new_one / correct_one / (jnp.sqrt(new_two / correct_two) + epsilon)
    new_master = master - learn_rate * (update + decay_rate * master)
    return (new_master, new_one, new_two)


def split_experts(flat_terms, experts_here, hidden_units):
    return jnp.stack(
        [
            flat_terms[:, index * hidden_units : (index + 1) * hidden_units]
            for index in range(experts_here)
        ],
        axis=0,
    )


def body(
    saved_hidden,
    routed_grad,
    expert_counts,
    block_starts,
    master_weights,
    first_moment,
    second_moment,
):
    model_width = routed_grad.shape[-1]
    hidden_units = saved_hidden.shape[-1]
    outgoing = routed_grad.reshape(-1, model_width)
    arrived = lax.all_to_all(outgoing, "exp", split_axis=0, concat_axis=0, tiled=True)
    hidden = saved_hidden.reshape(-1, hidden_units)
    row_total = hidden.shape[0]
    counts_local = expert_counts.reshape(-1)
    lower_row = block_starts.reshape(-1) * BLOCK
    upper_row = lower_row + counts_local
    experts_here = counts_local.shape[0]
    positions = lax.iota(jnp.int32, row_total)
    member = (positions[:, None] >= lower_row[None, :]) & (positions[:, None] < upper_row[None, :])
    masked = jnp.concatenate(
        [
            jnp.where(member[:, index : index + 1], hidden, jnp.zeros((), jnp.bfloat16))
            for index in range(experts_here)
        ],
        axis=1,
    )
    whole = split_experts(
        lax.dot_general(
            arrived, masked, (((0,), (0,)), ((), ())), preferred_element_type=jnp.float32
        ),
        experts_here,
        hidden_units,
    )
    inner = summed_on_arrival(whole.astype(jnp.bfloat16), "outer", 2)
    grad_part = summed_on_arrival(inner.astype(jnp.bfloat16), "rep", 1)
    new_master, new_first, new_second = adamw(
        grad_part, master_weights, first_moment, second_moment
    )
    updated = new_master.astype(jnp.bfloat16)
    along = gather_directly(updated, "rep", 1)
    new_weights = lax.all_gather(along, "outer", axis=2, tiled=True)
    return (new_master, new_first, new_second, new_weights)


def solution(mesh):
    in_specs = (
        P("outer", "rep", "exp", None),
        P("outer", "rep", "exp", None),
        P("outer", "rep", "exp"),
        P("outer", "rep", "exp"),
        P("exp", "rep", "outer"),
        P("exp", "rep", "outer"),
        P("exp", "rep", "outer"),
    )
    out_specs = (
        P("exp", "rep", "outer"),
        P("exp", "rep", "outer"),
        P("exp", "rep", "outer"),
        P("exp", None, None),
    )
    return jax.shard_map(body, mesh=mesh, in_specs=in_specs, out_specs=out_specs, check_vma=False)
```

profile of v0, /device:TPU:1, one launch (start us, length us, event | category | flops | bytes accessed | tf_op | source)
XLA Modules:
  0.0 259.8 jit_solution(15142603627902874229)
XLA Ops:
  7.2 0.0 copy-start.5
  7.2 0.0 copy-start.4
  7.2 0.0 copy-start
  7.2 15.8 %all-to-all-start = ((bf16[12,32,2048]{2,1,0:T(8,128)(2,1)}), bf16[12,32,2048]{2,1,0:T(8,128)(2,1)S(1)}, u32[]{:S(2)}, u32[]{:S(2)}) async-start(bf16[12,32,2048]{2,1,0:T(8,128)(2,1)} %bitcast.38), calls=%async_computation | async-start | bytes 3145728 | tf_op jit(solution)/shard_map/all_to_all | solution.py:76
  23.1 0.0 all-gather.2.cloned.1.call-start
  23.1 0.0 copy-done.5
  23.1 0.0 copy-done.4
  23.1 0.1 compare_and_fusion
  23.2 0.0 copy-done
  23.3 0.2 bitcast_select_fusion.1
  23.4 52.9 %all-to-all-done = bf16[12,32,2048]{2,1,0:T(8,128)(2,1)S(1)} async-done(((bf16[12,32,2048]{2,1,0:T(8,128)(2,1)}), bf16[12,32,2048]{2,1,0:T(8,128)(2,1)S(1)}, u32[]{:S(2)}, u32[]{:S(2)}) %all-to-all-start) | async-done | bytes 1572896 | tf_op jit(solution)/shard_map/all_to_all | solution.py:76
  76.3 2.4 convert_bitcast_fusion
  78.7 0.6 fusion.7
  79.3 0.4 maximum_bitcast_fusion
  79.7 58.7 %all_to_all.27 = bf16[4,2,2048,128]{2,3,1,0:T(8,128)(2,1)} all-to-all(bf16[4,2,2048,128]{2,3,1,0:T(8,128)(2,1)S(1)} %maximum_bitcast_fusion), channel_id=1, replica_groups=mesh['outer'=4,'rep'=16,'exp'=12] {'outer'}, dimensions={0} | all-to-all | bytes 8388608 | tf_op jit(solution)/shard_map/all_to_all | solution.py:26
  138.4 3.1 %reduce_sum.21 = bf16[2,2048,128]{1,2,0:T(8,128)(2,1)S(1)} reduce(bf16[4,2,2048,128]{2,3,1,0:T(8,128)(2,1)} %all_to_all.27, bf16[]{:T(256)} %constant.5.clone.1), dimensions={0}, to_apply=%region_0.1 | reduce | flops 1572864 | bytes 5242882 | tf_op jit(solution)/shard_map/reduce_sum | solution.py:27
  141.5 0.2 copy.21
  141.7 0.9 copy.18
  142.6 0.0 copy-start.1
  142.6 0.0 copy-start.2
  142.6 0.0 copy-start.3
  142.7 34.0 %all_to_all.28 = bf16[16,2,128,128]{3,2,1,0:T(8,128)(2,1)S(1)} all-to-all(bf16[16,2,128,128]{3,2,1,0:T(8,128)(2,1)S(1)} %bitcast.36), channel_id=1, replica_groups=mesh['outer'=4,'rep'=16,'exp'=12] {'rep'}, dimensions={0} | all-to-all | bytes 2097152 | tf_op jit(solution)/shard_map/all_to_all | solution.py:26
  176.6 0.1 convert_reduce_fusion
  176.8 0.0 copy-done.1
  176.8 0.0 copy-done.2
  176.8 0.8 fusion.5
  177.6 0.2 broadcast_in_dim.34
  177.8 31.0 %all_to_all.29 = bf16[16,2,128,128]{3,2,1,0:T(8,128)(2,1)S(1)} all-to-all(bf16[16,2,128,128]{3,2,1,0:T(8,128)(2,1)S(1)} %broadcast_in_dim.34), channel_id=1, replica_groups=mesh['outer'=4,'rep'=16,'exp'=12] {'rep'}, dimensions={0} | all-to-all | bytes 2097152 | tf_op jit(solution)/shard_map/all_to_all | solution.py:32
  208.9 1.0 copy.19
  209.9 0.0 all-gather.2.cloned.1.call-update
  210.0 38.5 %all-gather.2.cloned.1.call-done = bf16[2,2048,512]{2,1,0:T(8,128)(2,1)} async-done(((bf16[2,2048,128]{2,1,0:T(8,128)(2,1)}), bf16[2,2048,512]{2,1,0:T(8,128)(2,1)}) %all-gather.2.cloned.1.call-update) | async-done | bytes 4194320 | tf_op jit(solution)/shard_map/all_gather | solution.py:106
  248.5 4.5 %copy.23 = bf16[2,2048,512]{2,1,0:T(8,128)(2,1)} copy(bf16[2,2048,512]{2,1,0:T(8,128)(2,1)} %all-gather.2.cloned.1.call-done) | data formatting | bytes 8388608
  (4 shorter events, 0.0 us)
Async XLA Ops:
  7.2 15.9 %copy-start.5 = (s32[1,1,2]{2,1,0:T(1,128)S(1)}, s32[1,1,2]{2,1,0:T(1,128)}, u32[]{:S(2)}) copy-start(s32[1,1,2]{2,1,0:T(1,128)} %param.10) | copy-start | bytes 28
  7.2 15.9 %copy-start.4 = (s32[1,1,2]{2,1,0:T(1,128)S(1)}, s32[1,1,2]{2,1,0:T(1,128)}, u32[]{:S(2)}) copy-start(s32[1,1,2]{2,1,0:T(1,128)} %param.9) | copy-start | bytes 28
  7.2 16.1 %copy-start = (bf16[1,1,384,512]{3,2,1,0:T(8,128)(2,1)S(1)}, bf16[1,1,384,512]{3,2,1,0:T(8,128)(2,1)}, u32[]{:S(2)}) copy-start(bf16[1,1,384,512]{3,2,1,0:T(8,128)(2,1)} %param.7) | copy-start | bytes 1179652
  7.2 69.2 %all-to-all-start = ((bf16[12,32,2048]{2,1,0:T(8,128)(2,1)}), bf16[12,32,2048]{2,1,0:T(8,128)(2,1)S(1)}, u32[]{:S(2)}, u32[]{:S(2)}) async-start(bf16[12,32,2048]{2,1,0:T(8,128)(2,1)} %bitcast.38), calls=%async_computation | async-start | bytes 3145728 | tf_op jit(solution)/shard_map/all_to_all | solution.py:76
  23.1 225.4 %all-gather.2.cloned.1.call-start = ((), (), s32[]{:S(2)}) async-start(), calls=%async_computation.4 | async-start | bytes 5242880 | tf_op jit(solution)/shard_map/all_gather | solution.py:106
  142.6 34.2 %copy-start.1 = (f32[2,128,128]{2,1,0:T(8,128)S(1)}, f32[2,128,128]{2,1,0:T(8,128)}, u32[]{:S(2)}) copy-start(f32[2,128,128]{2,1,0:T(8,128)} %param.11) | copy-start | bytes 393220
  142.6 34.2 %copy-start.2 = (f32[2,128,128]{2,1,0:T(8,128)S(1)}, f32[2,128,128]{2,1,0:T(8,128)}, u32[]{:S(2)}) copy-start(f32[2,128,128]{2,1,0:T(8,128)} %param.12) | copy-start | bytes 393220
  142.6 34.2 %copy-start.3 = (f32[2,128,128]{2,1,0:T(8,128)S(1)}, f32[2,128,128]{2,1,0:T(8,128)}, u32[]{:S(2)}) copy-start(f32[2,128,128]{2,1,0:T(8,128)} %param.13) | copy-start | bytes 393220
Sparse Core Ops, SparseCore 0:
  210.1 38.3 all-gather.1
where the time goes:
time: 260 us
  blocking collectives  124 us (48%)
  waiting for transfers between devices  91.4 us (35%)
  starting transfers between devices  15.9 us (6%)
  between operations  14.2 us (5%)
  local copies, waits for them, and re-layouts  7.5 us (3%)
  other arithmetic  4.67 us (2%)
    all_to_all x2, blocking collectives, summed_on_arrival(): lax.all_to_all(parts, axis, split_axis=0, concat_axis=0, tiled=True)  92.7 us
    all_to_all x1, waiting for transfers between devices, body(): lax.all_to_all(outgoing, 'exp', split_axis=0, concat_axis=0, tiled=True)  52.9 us
    all_gather x1, waiting for transfers between devices, body(): new_weights = lax.all_gather(along, 'outer', axis=2, tiled=True)  38.5 us
    all_to_all x1, blocking collectives, sent_to_all(): return lax.all_to_all(copies, axis, split_axis=0, concat_axis=0, tiled=True)  31 us
    all_to_all x1, starting transfers between devices, body(): lax.all_to_all(outgoing, 'exp', split_axis=0, concat_axis=0, tiled=True)  15.8 us
  transfers between devices with their start and end apart: 2, of which 2 were waited for; matrix products, arithmetic and copies ran while one was open for 0% of the time, Pallas kernels for 0%

commit v1 on v0

v1 whole, which is shorter than its diff:
```python
import functools

import jax
import jax.numpy as jnp
from jax import lax
from jax.experimental import pallas as pl
from jax.experimental.pallas import tpu as pltpu
from jax.sharding import PartitionSpec as P

MESH = pl.DeviceIdType.MESH
BLOCK = 128
LANE = 128
SUB = 16
AHEAD = 2

beta_one = 0.9
beta_two = 0.95
learn_rate = 0.001
decay_rate = 0.1
epsilon = 1e-08
correct_one = 0.9999734386011124
correct_two = 0.994079470779666


def adamw(grad_part, master, moment_one, moment_two):
    new_one = beta_one * moment_one + (1.0 - beta_one) * grad_part
    new_two = beta_two * moment_two + (1.0 - beta_two) * grad_part * grad_part
    update = new_one / correct_one / (jnp.sqrt(new_two / correct_two) + epsilon)
    new_master = master - learn_rate * (update + decay_rate * master)
    return (new_master, new_one, new_two)


def kernel(
    n_y,
    n_z,
    counts_ref,
    starts_ref,
    hidden_hbm,
    grads_hbm,
    master_hbm,
    first_hbm,
    second_hbm,
    new_master,
    new_first,
    new_second,
    weights_hbm,
    grads,
    hidden,
    master,
    first,
    second,
    spread,
    outgoing,
    arrived,
    turned,
    partial,
    from_x,
    to_y,
    from_y,
    gathered,
    load_sem,
    turn_sem,
    z_send,
    z_recv,
    x_send,
    x_recv,
    y_send,
    y_recv,
    v_send,
    v_recv,
    u_send,
    u_recv,
    c_send,
    c_recv,
    out_sem,
):
    rows = grads.shape[0]
    slots = rows // n_z
    chunks = LANE // SUB
    outer = lax.axis_index("outer")
    rep = lax.axis_index("rep")
    z = lax.axis_index("exp")
    xh, c = outer // 2, outer % 2
    y, xl = rep // 2, rep % 2
    here = xh * 2 + xl

    def device(xh=xh, xl=xl, y=y, z=z, c=c):
        return (xh * 2 + c, y * 2 + xl, z)

    def push(src, dst, send_sem, recv_sem, target):
        pltpu.make_async_remote_copy(
            src_ref=src,
            dst_ref=dst,
            send_sem=send_sem,
            recv_sem=recv_sem,
            device_id=target,
            device_id_type=MESH,
        ).start()

    def take(like, sem):
        pltpu.make_async_copy(like, like, sem).wait()

    loads = [
        (grads_hbm.at[0, 0], grads),
        (hidden_hbm.at[0, 0], hidden),
        (master_hbm, master),
        (first_hbm, first),
        (second_hbm, second),
    ]
    for index, (src, dst) in enumerate(loads):
        pltpu.make_async_copy(src, dst, load_sem.at[index]).start()

    def loaded(index):
        pltpu.make_async_copy(*loads[index], load_sem.at[index]).wait()

    z_order = [n_z // 2]
    for step in range(n_z // 2 - 1, 0, -1):
        z_order += [step, n_z - step]
    barrier = pltpu.get_barrier_semaphore()
    peers = [device(z=lax.rem(z + dz, n_z), c=cc) for dz in z_order for cc in (0, 1)]
    peers += [device(c=1 - c)]
    peers += [
        device(xh=(xh + dh) % 2, xl=(xl + dl) % 2, c=cc)
        for dh, dl in ((0, 1), (1, 0), (1, 1))
        for cc in (0, 1)
    ]
    peers += [device(y=lax.rem(y + dy, n_y)) for dy in range(1, n_y)]
    for peer in peers:
        pl.semaphore_signal(barrier, inc=1, device_id=peer, device_id_type=MESH)

    row = lax.broadcasted_iota(jnp.int32, spread.shape, 0)
    lane = lax.broadcasted_iota(jnp.int32, spread.shape, 1)
    wanted = (lane % LANE) // SUB * (2 * LANE) + lane // LANE * LANE + lane % SUB
    spread[...] = jnp.where(row - (LANE - SUB) == wanted, 1.0, 0.0).astype(jnp.bfloat16)
    loaded(0)
    pl.semaphore_wait(barrier, len(peers))

    def send_grads(t):
        window = spread[pl.ds(pl.multiple_of((LANE - SUB) - SUB * t, SUB), grads.shape[1]), :]
        permuted = jnp.dot(grads[...], window, preferred_element_type=jnp.float32)
        permuted = permuted.astype(jnp.bfloat16)
        outgoing[t, 0] = permuted[:, :LANE]
        outgoing[t, 1] = permuted[:, LANE:]
        landing = pl.ds(pl.multiple_of(c * rows + z * slots, slots), slots)
        for dz in z_order:
            to = lax.rem(z + dz, n_z)
            leaving = pl.ds(pl.multiple_of(to * slots, slots), slots)
            for cc in (0, 1):
                push(
                    outgoing.at[t, cc, leaving],
                    arrived.at[t, landing],
                    z_send.at[t],
                    z_recv.at[t],
                    device(z=to, c=cc),
                )
        staying = pl.ds(pl.multiple_of(z * slots, slots), slots)
        push(
            outgoing.at[t, 1 - c, staying],
            arrived.at[t, landing],
            z_send.at[t],
            z_recv.at[t],
            device(c=1 - c),
        )
        pltpu.make_async_copy(
            outgoing.at[t, c, staying], arrived.at[t, landing], z_recv.at[t]
        ).start()

    def turn_hidden():
        loaded(1)
        position = lax.broadcasted_iota(jnp.int32, (LANE, rows), 1)
        for tile in range(4):
            flipped = hidden[:, tile * LANE : (tile + 1) * LANE].astype(jnp.float32).T
            for e in (0, 1):
                lower = starts_ref[0, 0, e] * BLOCK
                upper = lower + counts_ref[0, 0, e]
                kept = jnp.where((position >= lower) & (position < upper), flipped, 0.0)
                at = (tile * 2 + e) * LANE
                turned[c, at : at + LANE, :] = kept.astype(jnp.bfloat16)
        push(turned.at[c], turned.at[c], turn_sem.at[0], turn_sem.at[1], device(c=1 - c))
        for index in (2, 3, 4):
            loaded(index)
        take(turned.at[0], turn_sem.at[1])

    def multiply(t):
        take(arrived.at[t], z_recv.at[t])
        for piece in range(4):
            at = slice(piece * 2 * LANE, (piece + 1) * 2 * LANE)
            left = jnp.concatenate([turned[0, at, :], turned[1, at, :]], axis=1)
            product = jnp.dot(left, arrived[t], preferred_element_type=jnp.float32)
            partial[t, piece] = product.astype(jnp.bfloat16)
            th, tc = piece // 2, piece % 2
            mine = (xl == c) & (xh == th) & (c == tc)

            @pl.when(mine)
            def _():
                pltpu.make_async_copy(
                    partial.at[t, piece], from_x.at[t, here], x_recv.at[t]
                ).start()

            @pl.when(jnp.logical_not(mine))
            def _():
                push(
                    partial.at[t, piece],
                    from_x.at[t, here],
                    x_send.at[t],
                    x_recv.at[t],
                    device(xh=th, xl=c, c=tc),
                )

    def sum_x(t):
        take(from_x.at[t], x_recv.at[t])
        for e in (0, 1):
            at = slice(e * LANE, (e + 1) * LANE)
            total = from_x[t, 0, at, :].astype(jnp.float32)
            for source in range(1, 4):
                total += from_x[t, source, at, :].astype(jnp.float32)
            flat = total.T.astype(jnp.bfloat16)
            for to in range(n_y):
                to_y[t, to, e] = flat[to * SUB : (to + 1) * SUB, :]
        for dy in range(1, n_y):
            to = lax.rem(y + dy, n_y)
            push(to_y.at[t, to], from_y.at[t, y], y_send.at[t], y_recv.at[t], device(y=to))
        pltpu.make_async_copy(to_y.at[t, y], from_y.at[t, y], y_recv.at[t]).start()

    def update(t):
        take(from_y.at[t], y_recv.at[t])
        total = from_y[t, 0].astype(jnp.float32)
        for source in range(1, n_y):
            total += from_y[t, source].astype(jnp.float32)
        at = pl.ds(pl.multiple_of(t * SUB, SUB), SUB)
        one, two, three = adamw(total, master[:, at, :], first[:, at, :], second[:, at, :])
        new_master[:, at, :] = one
        new_first[:, at, :] = two
        new_second[:, at, :] = three
        gathered[t, c, here, :, y] = one.astype(jnp.bfloat16)
        block = gathered.at[t, c, here, :, y]
        for dy in range(1, n_y):
            push(block, block, v_send.at[t], v_recv.at[t], device(y=lax.rem(y + dy, n_y)))

    def gather_x(t):
        take(gathered.at[t, c, here, :, pl.ds(0, n_y - 1)], v_recv.at[t])
        block = gathered.at[t, c, here]
        for dh, dl in ((1, 1), (0, 1), (1, 0)):
            to = device(xh=(xh + dh) % 2, xl=(xl + dl) % 2)
            push(block, block, u_send.at[t], u_recv.at[t], to)

    def write_out(t, core):
        for tile in range(4):
            th, tl = tile // 2, tile % 2
            columns = pl.ds(pl.multiple_of((th * 2 + core) * LANE, LANE), LANE)
            pltpu.make_async_copy(
                gathered.at[t, core, tile],
                weights_hbm.at[:, :, tl, t, :, columns],
                out_sem.at[t],
            ).start()

    def cross(t):
        take(gathered.at[t, c, pl.ds(0, 3)], u_recv.at[t])
        block = gathered.at[t, c]
        push(block, block, c_send.at[t], c_recv.at[t], device(c=1 - c))
        write_out(t, c)

    def finish(t):
        take(gathered.at[t, c], c_recv.at[t])
        write_out(t, 1 - c)

    def at_step(s, delay, stage):
        @pl.when((s >= delay) & (s < delay + chunks))
        def _():
            stage((s + (2 * chunks - delay)) % chunks)

    def step(s, carry):
        at_step(s, 0, send_grads)

        @pl.when(s == AHEAD - 1)
        def _():
            turn_hidden()

        at_step(s, AHEAD, multiply)
        at_step(s, AHEAD + 1, update)
        at_step(s, AHEAD, sum_x)
        at_step(s, AHEAD + 2, cross)
        at_step(s, AHEAD + 1, gather_x)
        at_step(s, AHEAD + 2, finish)
        return carry

    lax.fori_loop(0, chunks + AHEAD + 2, step, 0)

    take(turned.at[0], turn_sem.at[0])

    def drain(t, carry):
        take(arrived.at[t, pl.ds(0, 2 * rows - slots)], z_send.at[t])

        @pl.when(xl == c)
        def _():
            take(from_x.at[t, pl.ds(0, 3)], x_send.at[t])

        @pl.when(xl != c)
        def _():
            take(from_x.at[t], x_send.at[t])

        take(from_y.at[t, pl.ds(0, n_y - 1)], y_send.at[t])
        take(from_y.at[t, pl.ds(0, n_y - 1)], v_send.at[t])
        take(gathered.at[t, c, pl.ds(0, 3)], u_send.at[t])
        take(gathered.at[t, c], c_send.at[t])
        take(gathered.at[t], out_sem.at[t])
        return carry

    lax.fori_loop(0, chunks, drain, 0)


def body(
    saved_hidden,
    routed_grad,
    expert_counts,
    block_starts,
    master_weights,
    first_moment,
    second_moment,
):
    rows, d = routed_grad.shape[2:]
    ff = saved_hidden.shape[3]
    n_y = lax.axis_size("rep") // 2
    n_z = lax.axis_size("exp")
    chunks = LANE // SUB
    shard = master_weights.shape
    bf16, f32 = jnp.bfloat16, jnp.float32
    smem = pl.BlockSpec(memory_space=pltpu.SMEM)
    vmem = pl.BlockSpec(memory_space=pltpu.VMEM)
    anywhere = pl.BlockSpec(memory_space=pl.ANY)
    sems = pltpu.SemaphoreType.DMA((chunks,))
    new_master, new_first, new_second, weights = pl.pallas_call(
        functools.partial(kernel, n_y, n_z),
        out_shape=[jax.ShapeDtypeStruct(shard, f32)] * 3
        + [jax.ShapeDtypeStruct((2, n_y, 2, chunks, SUB, ff), bf16)],
        in_specs=[smem, smem] + [anywhere] * 5,
        out_specs=[vmem] * 3 + [anywhere],
        scratch_shapes=[
            pltpu.VMEM((rows, d), bf16),
            pltpu.VMEM((rows, ff), bf16),
            pltpu.VMEM(shard, f32),
            pltpu.VMEM(shard, f32),
            pltpu.VMEM(shard, f32),
            pltpu.VMEM((d + LANE - SUB, 2 * LANE), bf16),
            pltpu.VMEM((chunks, 2, rows, LANE), bf16),
            pltpu.VMEM((chunks, 2 * rows, LANE), bf16),
            pltpu.VMEM((2, 2 * ff, rows), bf16),
            pltpu.VMEM((chunks, 4, 2 * LANE, LANE), bf16),
            pltpu.VMEM((chunks, 4, 2 * LANE, LANE), bf16),
            pltpu.VMEM((chunks, n_y, 2, SUB, LANE), bf16),
            pltpu.VMEM((chunks, n_y, 2, SUB, LANE), bf16),
            pltpu.VMEM((chunks, 2, 4, 2, n_y, SUB, LANE), bf16),
            pltpu.SemaphoreType.DMA((5,)),
            pltpu.SemaphoreType.DMA((2,)),
        ]
        + [sems] * 13,
        compiler_params=pltpu.CompilerParams(
            collective_id=0, has_side_effects=True, vmem_limit_bytes=40 << 20
        ),
        name="expert_update",
    )(
        expert_counts,
        block_starts,
        saved_hidden,
        routed_grad,
        master_weights,
        first_moment,
        second_moment,
    )
    return (new_master, new_first, new_second, weights.reshape(2, d, ff))


def solution(mesh):
    in_specs = (
        P("outer", "rep", "exp", None),
        P("outer", "rep", "exp", None),
        P("outer", "rep", "exp"),
        P("outer", "rep", "exp"),
        P("exp", "rep", "outer"),
        P("exp", "rep", "outer"),
        P("exp", "rep", "outer"),
    )
    out_specs = (
        P("exp", "rep", "outer"),
        P("exp", "rep", "outer"),
        P("exp", "rep", "outer"),
        P("exp", None, None),
    )
    return jax.shard_map(body, mesh=mesh, in_specs=in_specs, out_specs=out_specs, check_vma=False)
```

time: 260 us -> 128 us (0.49)
  blocking collectives: 124 us -> 0 us
  Pallas kernels: 0 us -> 117 us
  waiting for transfers between devices: 91.4 us -> 0 us
  starting transfers between devices: 15.9 us -> 0 us
  between operations: 14.2 us -> 0.66 us
  other arithmetic: 4.67 us -> 0 us
  local copies, waits for them, and re-layouts: 7.5 us -> 10.4 us
    all_to_all x3 -> x0, blocking collectives: 124 us -> none  [the longest x2 92.7 us: summed_on_arrival(): lax.all_to_all(parts, axis, split_axis=0, concat_axis=0, tiled=True)]
    pallas_call x0 -> x1, Pallas kernels: none -> 117 us  [body(): pl.pallas_call(functools.partial(kernel, n_y, n_z), out_shape=[jax.ShapeD...]
    all_to_all x1 -> x0, waiting for transfers between devices: 52.9 us -> none  [body(): lax.all_to_all(outgoing, 'exp', split_axis=0, concat_axis=0, tiled=True)]
    all_gather x1 -> x0, waiting for transfers between devices: 38.5 us -> none  [body(): new_weights = lax.all_gather(along, 'outer', axis=2, tiled=True)]
    all_to_all x1 -> x0, starting transfers between devices: 15.8 us -> none  [body(): lax.all_to_all(outgoing, 'exp', split_axis=0, concat_axis=0, tiled=True)]
    unnamed x14 -> x18, local copies, waits for them, and re-layouts: 4.73 us -> 10.4 us
    reduce_sum x2 -> x0, other arithmetic: 3.22 us -> none  [summed_on_arrival(): return arrived.astype(jnp.float32).sum(axis=0)]
  transfers between devices with their start and end apart: 2 -> 0, of which waited for: 2 -> 0; matrix products, arithmetic and copies ran while one was open for 0% -> 0% of each run, Pallas kernels for 0% -> 0%
where the time goes in v1:
time: 128 us
  Pallas kernels  117 us (91%)
  local copies, waits for them, and re-layouts  10.4 us (8%)
    pallas_call x1, Pallas kernels, body(): pl.pallas_call(functools.partial(kernel, n_y, n_z), out_shape=[jax.ShapeD...  117 us
    unnamed x18, local copies, waits for them, and re-layouts  10.4 us

profile of v1, /device:TPU:1, one launch (start us, length us, event | category | flops | bytes accessed | tf_op | source)
XLA Modules:
  0.0 128.0 jit_solution(14437584563725809027)
XLA Ops:
  0.6 0.0 copy-start
  0.6 1.4 %copy-done = bf16[1,1,384,2048]{3,2,1,0:T(8,128)(2,1)S(1)} copy-done((bf16[1,1,384,2048]{3,2,1,0:T(8,128)(2,1)S(1)}, bf16[1,1,384,2048]{3,2,1,0:T(8,128)(2,1)}, u32[]{:S(2)}) %copy-start) | copy-done | bytes 1572888
  2.0 0.0 copy-start.1
  2.0 1.0 copy-done.1
  3.0 0.0 copy-start.2
  3.0 0.9 copy-done.2
  3.9 0.0 copy-start.3
  3.9 0.9 copy-done.3
  4.8 0.0 copy-start.4
  4.8 0.9 copy-done.4
  5.8 0.0 copy-start.5
  5.8 0.7 copy-done.5
  6.4 0.0 copy-start.6
  6.4 0.7 copy-done.6
  7.1 116.9 %expert_update.1 = (f32[2,128,128]{2,1,0:T(8,128)S(1)}, f32[2,128,128]{2,1,0:T(8,128)S(1)}, f32[2,128,128]{2,1,0:T(8,128)S(1)}, bf16[2,8,2,8,16,512]{5,4,3,2,1,0:T(8,128)(2,1)S(1)}) custom-call(s32[1,1,2]{2,1,0:T(1,128)S(1)} %copy-done.5, s32[1,1,2]{2,1,0:T(1,128)S(1)} %copy-done.6, bf16[1,1,384,512]{3,2,1,0:T(8,128)(2,1)S(1)} %copy-done.1, ...), custom_call_target="tpu_custom_call" | custom-call | tf_op jit(solution)/shard_map/expert_update/pallas_call | solution.py:332
  124.0 0.7 copy.15
  124.7 0.7 copy.16
  125.3 0.7 copy.17
  126.0 2.0 %copy.18 = bf16[2,2048,512]{2,1,0:T(8,128)(2,1)} copy(bf16[2,2048,512]{2,1,0:T(8,128)(2,1)S(1)} %bitcast.1) | data formatting | bytes 8388608
Async XLA Ops:
  0.6 1.4 %copy-start = (bf16[1,1,384,2048]{3,2,1,0:T(8,128)(2,1)S(1)}, bf16[1,1,384,2048]{3,2,1,0:T(8,128)(2,1)}, u32[]{:S(2)}) copy-start(bf16[1,1,384,2048]{3,2,1,0:T(8,128)(2,1)} %grads_hbm.1) | copy-start | bytes 4718596
  2.0 1.0 copy-start.1
  3.0 0.9 copy-start.2
  3.9 0.9 copy-start.3
  4.8 0.9 copy-start.4
  5.8 0.7 copy-start.5
  6.4 0.7 copy-start.6

commit v2 on v1

--- a/solution.py
+++ b/solution.py
@@ -33,8 +33,8 @@
 def kernel(
     n_y,
     n_z,
-    counts_ref,
-    starts_ref,
+    counts_hbm,
+    starts_hbm,
     hidden_hbm,
     grads_hbm,
     master_hbm,
@@ -43,7 +43,9 @@
     new_master,
     new_first,
     new_second,
-    weights_hbm,
+    gathered,
+    counts,
+    starts,
     grads,
     hidden,
     master,
@@ -57,7 +59,6 @@
     from_x,
     to_y,
     from_y,
-    gathered,
     load_sem,
     turn_sem,
     z_send,
@@ -66,13 +67,16 @@
     x_recv,
     y_send,
     y_recv,
-    v_send,
-    v_recv,
-    u_send,
-    u_recv,
+    y_first_send,
+    y_first_recv,
+    x_first_send,
+    x_first_recv,
+    x_last_send,
+    x_last_recv,
+    y_last_send,
+    y_last_recv,
     c_send,
     c_recv,
-    out_sem,
 ):
     rows = grads.shape[0]
     slots = rows // n_z
@@ -106,6 +110,8 @@
         (master_hbm, master),
         (first_hbm, first),
         (second_hbm, second),
+        (counts_hbm, counts),
+        (starts_hbm, starts),
     ]
     for index, (src, dst) in enumerate(loads):
         pltpu.make_async_copy(src, dst, load_sem.at[index]).start()
@@ -113,6 +119,10 @@
     def loaded(index):
         pltpu.make_async_copy(*loads[index], load_sem.at[index]).wait()
 
+    y_peers = [device(y=lax.rem(y + dy, n_y)) for dy in range(1, n_y)]
+    x_peers = [
+        device(xh=(xh + dh) % 2, xl=(xl + dl) % 2) for dh, dl in ((1, 1), (0, 1), (1, 0))
+    ]
     z_order = [n_z // 2]
     for step in range(n_z // 2 - 1, 0, -1):
         z_order += [step, n_z - step]
@@ -124,14 +134,14 @@
         for dh, dl in ((0, 1), (1, 0), (1, 1))
         for cc in (0, 1)
     ]
-    peers += [device(y=lax.rem(y + dy, n_y)) for dy in range(1, n_y)]
+    peers += y_peers
     for peer in peers:
         pl.semaphore_signal(barrier, inc=1, device_id=peer, device_id_type=MESH)
 
     row = lax.broadcasted_iota(jnp.int32, spread.shape, 0)
-    lane = lax.broadcasted_iota(jnp.int32, spread.shape, 1)
-    wanted = (lane % LANE) // SUB * (2 * LANE) + lane // LANE * LANE + lane % SUB
-    spread[...] = jnp.where(row - (LANE - SUB) == wanted, 1.0, 0.0).astype(jnp.bfloat16)
+    lane = lax.broadcasted_iota(jnp.int32, (1, spread.shape[1]), 1)
+    wanted = (LANE - SUB) + (lane % LANE) // SUB * (2 * LANE) + lane // LANE * LANE + lane % SUB
+    spread[...] = jnp.where(row == wanted, 1.0, 0.0).astype(jnp.bfloat16)
     loaded(0)
     pl.semaphore_wait(barrier, len(peers))
 
@@ -166,13 +176,14 @@
         ).start()
 
     def turn_hidden():
-        loaded(1)
+        for index in (1, 5, 6):
+            loaded(index)
         position = lax.broadcasted_iota(jnp.int32, (LANE, rows), 1)
         for tile in range(4):
             flipped = hidden[:, tile * LANE : (tile + 1) * LANE].astype(jnp.float32).T
             for e in (0, 1):
-                lower = starts_ref[0, 0, e] * BLOCK
-                upper = lower + counts_ref[0, 0, e]
+                lower = starts[0, :, e : e + 1] * BLOCK
+                upper = lower + counts[0, :, e : e + 1]
                 kept = jnp.where((position >= lower) & (position < upper), flipped, 0.0)
                 at = (tile * 2 + e) * LANE
                 turned[c, at : at + LANE, :] = kept.astype(jnp.bfloat16)
@@ -232,37 +243,30 @@
         new_master[:, at, :] = one
         new_first[:, at, :] = two
         new_second[:, at, :] = three
-        gathered[t, c, here, :, y] = one.astype(jnp.bfloat16)
-        block = gathered.at[t, c, here, :, y]
-        for dy in range(1, n_y):
-            push(block, block, v_send.at[t], v_recv.at[t], device(y=lax.rem(y + dy, n_y)))
-
-    def gather_x(t):
-        take(gathered.at[t, c, here, :, pl.ds(0, n_y - 1)], v_recv.at[t])
-        block = gathered.at[t, c, here]
-        for dh, dl in ((1, 1), (0, 1), (1, 0)):
-            to = device(xh=(xh + dh) % 2, xl=(xl + dl) % 2)
-            push(block, block, u_send.at[t], u_recv.at[t], to)
-
-    def write_out(t, core):
-        for tile in range(4):
-            th, tl = tile // 2, tile % 2
-            columns = pl.ds(pl.multiple_of((th * 2 + core) * LANE, LANE), LANE)
-            pltpu.make_async_copy(
-                gathered.at[t, core, tile],
-                weights_hbm.at[:, :, tl, t, :, columns],
-                out_sem.at[t],
-            ).start()
+        for e in (0, 1):
+            gathered[c, here, e, y, t] = one[e].astype(jnp.bfloat16)
+        along_y = gathered.at[c, here, 0, y, t]
+        along_x = gathered.at[c, here, 1, y, t]
+        for to in y_peers:
+            push(along_y, along_y, y_first_send.at[t], y_first_recv.at[t], to)
+        for to in x_peers:
+            push(along_x, along_x, x_first_send.at[t], x_first_recv.at[t], to)
+
+    def gather(t):
+        take(gathered.at[c, here, 0, pl.ds(0, n_y - 1), t], y_first_recv.at[t])
+        along_x = gathered.at[c, here, 0, :, t]
+        for to in x_peers:
+            push(along_x, along_x, x_last_send.at[t], x_last_recv.at[t], to)
+        take(gathered.at[c, pl.ds(0, 3), 1, y, t], x_first_recv.at[t])
+        along_y = gathered.at[c, :, 1, y, t]
+        for to in y_peers:
+            push(along_y, along_y, y_last_send.at[t], y_last_recv.at[t], to)
 
     def cross(t):
-        take(gathered.at[t, c, pl.ds(0, 3)], u_recv.at[t])
-        block = gathered.at[t, c]
+        take(gathered.at[c, pl.ds(0, 3), 0, :, t], x_last_recv.at[t])
+        take(gathered.at[c, :, 1, pl.ds(0, n_y - 1), t], y_last_recv.at[t])
+        block = gathered.at[c, :, :, :, t]
         push(block, block, c_send.at[t], c_recv.at[t], device(c=1 - c))
-        write_out(t, c)
-
-    def finish(t):
-        take(gathered.at[t, c], c_recv.at[t])
-        write_out(t, 1 - c)
 
     def at_step(s, delay, stage):
         @pl.when((s >= delay) & (s < delay + chunks))
@@ -270,21 +274,20 @@
             stage((s + (2 * chunks - delay)) % chunks)
 
     def step(s, carry):
+        at_step(s, AHEAD, multiply)
         at_step(s, 0, send_grads)
 
         @pl.when(s == AHEAD - 1)
         def _():
             turn_hidden()
 
-        at_step(s, AHEAD, multiply)
-        at_step(s, AHEAD + 1, update)
-        at_step(s, AHEAD, sum_x)
-        at_step(s, AHEAD + 2, cross)
-        at_step(s, AHEAD + 1, gather_x)
-        at_step(s, AHEAD + 2, finish)
+        at_step(s, AHEAD + 1, sum_x)
+        at_step(s, AHEAD + 2, update)
+        at_step(s, AHEAD + 3, gather)
+        at_step(s, AHEAD + 4, cross)
         return carry
 
-    lax.fori_loop(0, chunks + AHEAD + 2, step, 0)
+    lax.fori_loop(0, chunks + AHEAD + 4, step, 0)
 
     take(turned.at[0], turn_sem.at[0])
 
@@ -300,13 +303,33 @@
             take(from_x.at[t], x_send.at[t])
 
         take(from_y.at[t, pl.ds(0, n_y - 1)], y_send.at[t])
-        take(from_y.at[t, pl.ds(0, n_y - 1)], v_send.at[t])
-        take(gathered.at[t, c, pl.ds(0, 3)], u_send.at[t])
-        take(gathered.at[t, c], c_send.at[t])
-        take(gathered.at[t], out_sem.at[t])
+        take(gathered.at[c, here, 0, pl.ds(0, n_y - 1), t], y_first_send.at[t])
+        take(gathered.at[c, pl.ds(0, 3), 1, y, t], x_first_send.at[t])
+        take(gathered.at[c, pl.ds(0, 3), 0, :, t], x_last_send.at[t])
+        take(gathered.at[c, :, 1, pl.ds(0, n_y - 1), t], y_last_send.at[t])
+        take(gathered.at[c, :, :, :, t], c_send.at[t])
+        take(gathered.at[c, :, :, :, t], c_recv.at[t])
         return carry
 
     lax.fori_loop(0, chunks, drain, 0)
+
+
+def write_kernel(master, first, second, gathered, master_out, first_out, second_out, weights, sem):
+    copies = []
+    for core in (0, 1):
+        for tile in range(4):
+            th, tl = tile // 2, tile % 2
+            at = (th * 2 + core) * LANE
+            copies.append((gathered.at[core, tile], weights.at[:, :, tl, :, :, at : at + LANE]))
+    copies += [(master, master_out), (first, first_out), (second, second_out)]
+    started = [
+        pltpu.make_async_copy(src, dst, sem.at[index])
+        for index, (src, dst) in enumerate(copies)
+    ]
+    for copy in started:
+        copy.start()
+    for copy in started:
+        copy.wait()
 
 
 def body(
@@ -325,17 +348,18 @@
     chunks = LANE // SUB
     shard = master_weights.shape
     bf16, f32 = jnp.bfloat16, jnp.float32
-    smem = pl.BlockSpec(memory_space=pltpu.SMEM)
     vmem = pl.BlockSpec(memory_space=pltpu.VMEM)
-    anywhere = pl.BlockSpec(memory_space=pl.ANY)
+    hbm = pl.BlockSpec(memory_space=pltpu.HBM)
     sems = pltpu.SemaphoreType.DMA((chunks,))
-    new_master, new_first, new_second, weights = pl.pallas_call(
+    shards = [jax.ShapeDtypeStruct(shard, f32)] * 3
+    results = pl.pallas_call(
         functools.partial(kernel, n_y, n_z),
-        out_shape=[jax.ShapeDtypeStruct(shard, f32)] * 3
-        + [jax.ShapeDtypeStruct((2, n_y, 2, chunks, SUB, ff), bf16)],
-        in_specs=[smem, smem] + [anywhere] * 5,
-        out_specs=[vmem] * 3 + [anywhere],
+        out_shape=shards + [jax.ShapeDtypeStruct((2, 4, 2, n_y, chunks, SUB, LANE), bf16)],
+        in_specs=[hbm] * 7,
+        out_specs=[vmem] * 4,
         scratch_shapes=[
+            pltpu.VMEM(expert_counts.shape, jnp.int32),
+            pltpu.VMEM(block_starts.shape, jnp.int32),
             pltpu.VMEM((rows, d), bf16),
             pltpu.VMEM((rows, ff), bf16),
             pltpu.VMEM(shard, f32),
@@ -349,24 +373,32 @@
             pltpu.VMEM((chunks, 4, 2 * LANE, LANE), bf16),
             pltpu.VMEM((chunks, n_y, 2, SUB, LANE), bf16),
             pltpu.VMEM((chunks, n_y, 2, SUB, LANE), bf16),
-            pltpu.VMEM((chunks, 2, 4, 2, n_y, SUB, LANE), bf16),
-            pltpu.SemaphoreType.DMA((5,)),
+            pltpu.SemaphoreType.DMA((7,)),
             pltpu.SemaphoreType.DMA((2,)),
         ]
-        + [sems] * 13,
+        + [sems] * 16,
         compiler_params=pltpu.CompilerParams(
             collective_id=0, has_side_effects=True, vmem_limit_bytes=40 << 20
         ),
         name="expert_update",
     )(
-        expert_counts,
-        block_starts,
-        saved_hidden,
-        routed_grad,
-        master_weights,
-        first_moment,
-        second_moment,
+        pltpu.with_memory_space_constraint(expert_counts, pltpu.HBM),
+        pltpu.with_memory_space_constraint(block_starts, pltpu.HBM),
+        pltpu.with_memory_space_constraint(saved_hidden, pltpu.HBM),
+        pltpu.with_memory_space_constraint(routed_grad, pltpu.HBM),
+        pltpu.with_memory_space_constraint(master_weights, pltpu.HBM),
+        pltpu.with_memory_space_constraint(first_moment, pltpu.HBM),
+        pltpu.with_memory_space_constraint(second_moment, pltpu.HBM),
     )
+    new_master, new_first, new_second, weights = pl.pallas_call(
+        write_kernel,
+        out_shape=shards + [jax.ShapeDtypeStruct((2, n_y, 2, chunks, SUB, ff), bf16)],
+        in_specs=[vmem] * 4,
+        out_specs=[hbm] * 4,
+        scratch_shapes=[pltpu.SemaphoreType.DMA((11,))],
+        compiler_params=pltpu.CompilerParams(vmem_limit_bytes=16 << 20),
+        name="write_results",
+    )(*results)
     return (new_master, new_first, new_second, weights.reshape(2, d, ff))
 
 

time: 128 us -> 102 us (0.80)
  Pallas kernels: 117 us -> 101 us
  local copies, waits for them, and re-layouts: 10.4 us -> 0 us
    pallas_call x1 -> x2, Pallas kernels: 117 us -> 101 us  [the longest x1 99 us: body(): pl.pallas_call(functools.partial(kernel, n_y, n_z), out_shape=shards + [j...]
    unnamed x18 -> x0, local copies, waits for them, and re-layouts: 10.4 us -> none
where the time goes in v2:
time: 102 us
  Pallas kernels  101 us (99%)
    pallas_call x1, Pallas kernels, body(): pl.pallas_call(functools.partial(kernel, n_y, n_z), out_shape=shards + [j...  99 us
    pallas_call x1, Pallas kernels, body(): pl.pallas_call(write_kernel, out_shape=shards + [jax.ShapeDtypeStruct((2,...  2.21 us

profile of v2, /device:TPU:1, one launch (start us, length us, event | category | flops | bytes accessed | tf_op | source)
XLA Modules:
  0.0 101.9 jit_solution(16494294142264640546)
XLA Ops:
  0.6 99.0 %expert_update.1 = (f32[2,128,128]{2,1,0:T(8,128)S(1)}, f32[2,128,128]{2,1,0:T(8,128)S(1)}, f32[2,128,128]{2,1,0:T(8,128)S(1)}, bf16[2,4,2,8,8,16,128]{6,5,4,3,2,1,0:T(8,128)(2,1)S(1)}) custom-call(s32[1,1,2]{2,1,0:T(1,128)} %counts_hbm.1, s32[1,1,2]{2,1,0:T(1,128)} %starts_hbm.1, bf16[1,1,384,512]{3,2,1,0:T(8,128)(2,1)} %hidden_hbm.1, ...), custom_call_target="tpu_custom_call" | custom-call | tf_op jit(solution)/shard_map/expert_update/pallas_call | solution.py:355
  99.7 2.2 %write_results.1 = (f32[2,128,128]{2,1,0:T(8,128)}, f32[2,128,128]{2,1,0:T(8,128)}, f32[2,128,128]{2,1,0:T(8,128)}, bf16[2,8,2,8,16,512]{5,4,3,2,1,0:T(8,128)(2,1)}) custom-call(f32[2,128,128]{2,1,0:T(8,128)S(1)} %get-tuple-element.12.master, f32[2,128,128]{2,1,0:T(8,128)S(1)} %get-tuple-element.13.first, f32[2,128,128]{2,1,0:T(8,128)S(1)} %get-tuple-element.14.second, ...), custom_call_target="tpu_custom_call" | custom-call | tf_op jit(solution)/shard_map/write_results/pallas_call | solution.py:393

commit v3 on v2

--- a/solution.py
+++ b/solution.py
@@ -11,7 +11,7 @@
 BLOCK = 128
 LANE = 128
 SUB = 16
-AHEAD = 2
+AHEAD = 4
 
 beta_one = 0.9
 beta_two = 0.95
@@ -142,15 +142,19 @@
     lane = lax.broadcasted_iota(jnp.int32, (1, spread.shape[1]), 1)
     wanted = (LANE - SUB) + (lane % LANE) // SUB * (2 * LANE) + lane // LANE * LANE + lane % SUB
     spread[...] = jnp.where(row == wanted, 1.0, 0.0).astype(jnp.bfloat16)
-    loaded(0)
-    pl.semaphore_wait(barrier, len(peers))
-
-    def send_grads(t):
+
+    def permute(t):
         window = spread[pl.ds(pl.multiple_of((LANE - SUB) - SUB * t, SUB), grads.shape[1]), :]
         permuted = jnp.dot(grads[...], window, preferred_element_type=jnp.float32)
         permuted = permuted.astype(jnp.bfloat16)
         outgoing[t, 0] = permuted[:, :LANE]
         outgoing[t, 1] = permuted[:, LANE:]
+
+    loaded(0)
+    permute(0)
+    pl.semaphore_wait(barrier, len(peers))
+
+    def send_grads(t):
         landing = pl.ds(pl.multiple_of(c * rows + z * slots, slots), slots)
         for dz in z_order:
             to = lax.rem(z + dz, n_z)
@@ -277,6 +281,10 @@
         at_step(s, AHEAD, multiply)
         at_step(s, 0, send_grads)
 
+        @pl.when(s < chunks - 1)
+        def _():
+            permute((s + 1) % chunks)
+
         @pl.when(s == AHEAD - 1)
         def _():
             turn_hidden()
@@ -284,10 +292,10 @@
         at_step(s, AHEAD + 1, sum_x)
         at_step(s, AHEAD + 2, update)
         at_step(s, AHEAD + 3, gather)
-        at_step(s, AHEAD + 4, cross)
+        at_step(s, AHEAD + 5, cross)
         return carry
 
-    lax.fori_loop(0, chunks + AHEAD + 4, step, 0)
+    lax.fori_loop(0, chunks + AHEAD + 5, step, 0)
 
     take(turned.at[0], turn_sem.at[0])
 

time: 102 us -> 101 us (level)
    pallas_call x1, Pallas kernels: 99 us -> 97.8 us  [body(): pl.pallas_call(functools.partial(kernel, n_y, n_z), out_shape=shards + [j...]
where the time goes in v3:
time: 101 us
  Pallas kernels  100 us (99%)
    pallas_call x1, Pallas kernels, body(): pl.pallas_call(functools.partial(kernel, n_y, n_z), out_shape=shards + [j...  97.8 us
    pallas_call x1, Pallas kernels, body(): pl.pallas_call(write_kernel, out_shape=shards + [jax.ShapeDtypeStruct((2,...  2.21 us

profile of v3, /device:TPU:1, one launch (start us, length us, event | category | flops | bytes accessed | tf_op | source)
XLA Modules:
  0.0 100.7 jit_solution(8428323021327595758)
XLA Ops:
  0.6 97.8 %expert_update.1 = (f32[2,128,128]{2,1,0:T(8,128)S(1)}, f32[2,128,128]{2,1,0:T(8,128)S(1)}, f32[2,128,128]{2,1,0:T(8,128)S(1)}, bf16[2,4,2,8,8,16,128]{6,5,4,3,2,1,0:T(8,128)(2,1)S(1)}) custom-call(s32[1,1,2]{2,1,0:T(1,128)} %counts_hbm.1, s32[1,1,2]{2,1,0:T(1,128)} %starts_hbm.1, bf16[1,1,384,512]{3,2,1,0:T(8,128)(2,1)} %hidden_hbm.1, ...), custom_call_target="tpu_custom_call" | custom-call | tf_op jit(solution)/shard_map/expert_update/pallas_call | solution.py:363
  98.4 2.2 %write_results.1 = (f32[2,128,128]{2,1,0:T(8,128)}, f32[2,128,128]{2,1,0:T(8,128)}, f32[2,128,128]{2,1,0:T(8,128)}, bf16[2,8,2,8,16,512]{5,4,3,2,1,0:T(8,128)(2,1)}) custom-call(f32[2,128,128]{2,1,0:T(8,128)S(1)} %get-tuple-element.12.master, f32[2,128,128]{2,1,0:T(8,128)S(1)} %get-tuple-element.13.first, f32[2,128,128]{2,1,0:T(8,128)S(1)} %get-tuple-element.14.second, ...), custom_call_target="tpu_custom_call" | custom-call | tf_op jit(solution)/shard_map/write_results/pallas_call | solution.py:401
